TPU v7x, 32 devices: a whole 2x2x4 slice. The times are simulated.
32 devices in a mesh: seq: 8 (over z, x), head: 4 (over y, core).
Axes of the slice: x: 2, y: 2, z: 4, core: 2. Of those that a mesh axis runs over, the one named last changes fastest.
Arguments:
- xs: bfloat16 [12288, 1280], P('seq', 'head'), may hold values from -6 to 6
- dxs: bfloat16 [12288, 1280], P('seq', 'head'), may hold values from -6 to 6
- zgate: bfloat16 [12288, 1280], P('seq', 'head'), may hold values from -6 to 6
- bmat: bfloat16 [12288, 128], P('seq'), may hold values from -1 to 1
- cmat: bfloat16 [12288, 128], P('seq'), may hold values from -1 to 1
- dt_raw: float32 [20, 12288], P('head', 'seq'), may hold values from -3 to 3
- dt_bias: float32 [20], P('head'), may hold values from -1 to 1
- a_rate: float32 [20], P('head'), may hold values from 0 to 1, as said below
- d_skip: float32 [20], P('head'), may hold values from 0.5 to 2
- gain: float32 [1280], replicated, may hold values from 0.5 to 1.5
- traj_ids: int32 [48], P('seq'), may hold values from 0 to 3, as said below
Outputs:
- normed: bfloat16 [12288, 1280], P(('seq', 'head'))
- normed_tan: bfloat16 [12288, 1280], P(('seq', 'head'))
Inputs may be any that keep to these rules, and one draw needn't show every extreme that they name: `traj_ids`: never falling from one block to the next; trajectory 0 spans exactly the first 24 blocks, trajectory 1 the next 6 blocks or more, every other trajectory one block or more. `a_rate`: positive.
All inputs are finite; a program needn't handle non-finite values.
Results may differ from a plain program's by a relative error of at most 0.0057.
Values may be sent and summed in bfloat16 or wider, within the bound.
A program may use at most 128 MiB of HBM per device.

v0:
```python
import functools

import jax
import jax.numpy as jnp
from jax import lax
from jax.experimental import pallas as pl
from jax.experimental.pallas import tpu as pltpu
from jax.sharding import PartitionSpec as P

Q = 256
HALF = 128
TAIL = 16
MESH = pl.DeviceIdType.MESH
F32 = jnp.float32
BF16 = jnp.bfloat16


def column_of(ref, count):
    place = lax.broadcasted_iota(jnp.int32, (8, 1), 0)
    column = jnp.zeros((8, 1), F32)
    for h in range(count):
        column = jnp.where(place == h, ref[h], column)
    return column


def by_rows(one, two):
    return lax.dot_general(one, two, (((1,), (1,)), ((), ())), preferred_element_type=F32)


def kernel(
    n_seq, n_head, heads, blocks, rows,
    xs_hbm, dxs_hbm, zg_hbm, bm_hbm, cm_hbm, dt_hbm, bias_hbm, rate_hbm, skip_hbm, gain_hbm, traj_hbm,
    out_main, out_tan,
    xs, dxs, zg, bm, cm, dt, bias, rate, skip, gain, traj, in_sem,
    dt8, bstate, lrow, wrow, erow, lcol, dec, table, part, scale, smsg, sgot, enter, gsend, got,
    s_send, s_recv, g_send, g_recv, own_sem,
):
    chain = n_seq // 2
    seq = lax.axis_index("seq")
    me = lax.axis_index("head")
    rank = lax.rem(seq, chain)
    base = seq - rank

    fetches = [
        pltpu.make_async_copy(source, target, in_sem.at[i])
        for i, (source, target) in enumerate((
            (dt_hbm, dt), (bias_hbm, bias), (rate_hbm, rate), (xs_hbm, xs), (dxs_hbm, dxs),
            (bm_hbm, bm), (traj_hbm, traj), (cm_hbm, cm), (zg_hbm, zg), (skip_hbm, skip),
            (gain_hbm, gain),
        ))
    ]
    for fetch in fetches:
        fetch.start()

    barrier = pltpu.get_barrier_semaphore()
    for o in range(1, n_head):
        pl.semaphore_signal(
            barrier, inc=1, device_id=(seq, lax.rem(me + o, n_head)), device_id_type=MESH
        )
    for o in range(1, chain):
        pl.semaphore_signal(
            barrier, inc=1, device_id=(base + lax.rem(rank + o, chain), me), device_id_type=MESH
        )

    dt8[...] = jnp.zeros(dt8.shape, F32)
    for fetch in fetches[0:3]:
        fetch.wait()
    dt8[0:heads, :] = dt[...]
    step_all = jax.nn.softplus(dt8[...] + column_of(bias, heads))
    fall_all = step_all * column_of(rate, heads)
    step = jnp.concatenate([step_all[:, c * Q:(c + 1) * Q] for c in range(blocks)], axis=0)
    fall = jnp.concatenate([fall_all[:, c * Q:(c + 1) * Q] for c in range(blocks)], axis=0)
    first = fall.astype(BF16)
    rest = fall - first.astype(F32)
    second = rest.astype(BF16)
    third = (rest - second.astype(F32)).astype(BF16)
    upper = (
        lax.broadcasted_iota(jnp.int32, (Q, Q), 0) <= lax.broadcasted_iota(jnp.int32, (Q, Q), 1)
    ).astype(F32).astype(BF16)
    sums = [jnp.dot(x, upper, preferred_element_type=F32) for x in (first, second, third)]
    log_decay = -(sums[0] + (sums[1] + sums[2]))
    end_log = log_decay[:, Q - 1:Q]
    weight_in = step * jnp.exp(end_log - log_decay)
    end_wide = jnp.broadcast_to(end_log, (blocks * 8, 128))
    end_decay = jnp.exp(end_wide)
    whole_log = end_wide[0:8]
    for c in range(1, blocks):
        whole_log = whole_log + end_wide[c * 8:(c + 1) * 8]
    factor = jnp.exp(whole_log)
    for c in range(blocks):
        wrow[c] = weight_in[c * 8:(c + 1) * 8]
        dec[c] = end_decay[c * 8:(c + 1) * 8]

    def keep_after(c):
        return jnp.where(traj[c] == traj[c + 1], 1.0, 0.0).astype(F32)

    def values_of(h, c):
        low, at = h * 64, slice(c * Q, (c + 1) * Q)
        return jnp.concatenate([xs[low:low + 64, at], dxs[low:low + 64, at]], axis=0)

    def s_copy(h, d, to):
        return pltpu.make_async_remote_copy(
            src_ref=smsg.at[h],
            dst_ref=sgot.at[d - 1, h],
            send_sem=s_send.at[d - 1, h],
            recv_sem=s_recv.at[d - 1, h],
            device_id=(to, me),
            device_id_type=MESH,
        )

    for fetch in fetches[3:7]:
        fetch.wait()
    last_id = traj[blocks - 1].astype(F32)
    tail_row = lax.broadcasted_iota(jnp.int32, (TAIL, 128), 0)
    for h in range(heads):
        state = None
        for c in range(blocks):
            weighted = (values_of(h, c).astype(F32) * wrow[c, h:h + 1, :]).astype(BF16)
            block = jnp.dot(weighted, bm[c * Q:(c + 1) * Q, :], preferred_element_type=F32)
            bstate[h, c] = block
            if c == 0:
                state = block
            else:
                state = keep_after(c - 1) * (dec[c, h:h + 1, :] * state) + block
        smsg[h, 0:128, :] = state.astype(BF16)
        whole = jnp.broadcast_to(factor[h:h + 1, :], (TAIL, 128))
        high = whole.astype(BF16).astype(F32)
        tail = jnp.where(tail_row == 0, high, jnp.where(tail_row == 1, whole - high, last_id))
        smsg[h, 128:128 + TAIL, :] = tail.astype(BF16)
        if h == 0:
            pl.semaphore_wait(barrier, (n_head - 1) + (chain - 1))
        for d in range(chain - 1, 0, -1):
            @pl.when(rank + d < chain)
            def _():
                s_copy(h, d, seq + d).start()

    for fetch in fetches[7:]:
        fetch.wait()
    log_row = log_decay - jnp.log(step)
    decay = jnp.exp(log_decay)
    turned = jnp.concatenate([log_decay, jnp.zeros((128 - blocks * 8, Q), F32)], axis=0).T
    row_at = lax.broadcasted_iota(jnp.int32, (Q, Q), 0)
    col_at = lax.broadcasted_iota(jnp.int32, (Q, Q), 1)
    causal = row_at >= col_at
    for c in range(blocks):
        lrow[c] = log_row[c * 8:(c + 1) * 8]
        erow[c] = decay[c * 8:(c + 1) * 8]
        lcol[c] = turned[:, c * 8:(c + 1) * 8]
        at = slice(c * Q, (c + 1) * Q)
        table[c] = jnp.where(causal, by_rows(cm[at, :], bm[at, :]), 0.0)

    def g_copy(h, o, i):
        to = lax.rem(me + o, n_head)
        return pltpu.make_async_remote_copy(
            src_ref=gsend.at[h, pl.ds(pl.multiple_of(to * rows + i * span, 16), span), :],
            dst_ref=got.at[me, h, pl.ds(i * span, span), :],
            send_sem=g_send.at[o - 1, h, i],
            recv_sem=g_recv.at[o - 1, h, i],
            device_id=(seq, to),
            device_id_type=MESH,
        )

    def own_copy(h):
        return pltpu.make_async_copy(
            gsend.at[h, pl.ds(pl.multiple_of(me * rows, 16), rows), :], got.at[me, h], own_sem.at[h]
        )

    span = 128 if rows % 128 == 0 else rows
    pieces = rows // span
    order = sorted(range(1, n_head), key=lambda o: abs(o - n_head // 2))
    first_id = traj[0].astype(F32)
    for h in range(heads):
        low = h * 64
        for c in range(blocks):
            at = slice(c * Q, (c + 1) * Q)
            row = lrow[c, h:h + 1, :]
            wide = jnp.broadcast_to(lcol[c, :, h:h + 1], (Q, HALF))
            gate_in = zg[low:low + 64, at].astype(F32)
            gate = gate_in / (1.0 + jnp.exp(-gate_in))
            w_top = table[c, 0:HALF, 0:HALF] * jnp.exp(
                jnp.minimum(wide[0:HALF] - row[:, 0:HALF], 4.0)
            )
            w_left = table[c, HALF:Q, 0:HALF] * jnp.exp(wide[HALF:Q] - row[:, 0:HALF])
            w_corner = table[c, HALF:Q, HALF:Q] * jnp.exp(
                jnp.minimum(wide[HALF:Q] - row[:, HALF:Q], 4.0)
            )
            w_low = jnp.concatenate([w_left.astype(BF16), w_corner.astype(BF16)], axis=1)
            values = values_of(h, c)
            y = jnp.concatenate(
                [by_rows(values[:, 0:HALF], w_top.astype(BF16)), by_rows(values, w_low)], axis=1
            )
            y = y + skip[h] * values.astype(F32)
            part[c] = y * jnp.concatenate([gate, gate], axis=0)
            scale[c] = erow[c, h:h + 1, :] * gate

        enter[...] = jnp.zeros(enter.shape, F32)
        for d in range(chain - 1, 0, -1):
            @pl.when(rank >= d)
            def _():
                s_copy(h, d, seq - d).wait_recv()
                tail = sgot[d - 1, h, 128:128 + TAIL, :].astype(F32)
                passed = tail[0:1] + tail[1:2]
                same = jnp.where(tail[2:3] == first_id, 1.0, 0.0)
                enter[...] = passed * enter[...] + same * sgot[d - 1, h, 0:128, :].astype(F32)
        state = enter[...]
        for c in range(blocks):
            at = slice(c * Q, (c + 1) * Q)
            carried = by_rows(state.astype(BF16), cm[at, :])
            scaled = scale[c]
            gated = part[c] + carried * jnp.concatenate([scaled, scaled], axis=0)
            gsend[h, at, :] = gated.T.astype(BF16)
            if c < blocks - 1:
                state = keep_after(c) * (dec[c, h:h + 1, :] * state + bstate[h, c])
        own_copy(h).start()
        if h < heads - 2:
            for o in order:
                for i in range(pieces):
                    g_copy(h, o, i).start()
    for i in range(pieces):
        for h in range(heads - 2, heads):
            for o in order:
                g_copy(h, o, i).start()

    for h in range(heads):
        own_copy(h).wait()

    pairs = n_head * heads // 2
    width = n_head * heads * 64
    step_rows = 32
    left_lanes = lax.broadcasted_iota(jnp.int32, (step_rows, 128), 1) < 64

    def norm(i, carry):
        at = pl.ds(pl.multiple_of(i * step_rows, step_rows), step_rows)
        square = jnp.zeros((step_rows, 128), F32)
        cross = jnp.zeros((step_rows, 128), F32)
        for j in range(pairs):
            k, m = 2 * j, 2 * j + 1
            one = got[k // heads, k % heads, at, :].astype(F32)
            two = got[m // heads, m % heads, at, :].astype(F32)
            main = jnp.where(left_lanes, one, pltpu.roll(two, 64, 1))
            tan = jnp.where(left_lanes, pltpu.roll(one, 64, 1), two)
            square += main * main
            cross += main * tan
            out_main[at, j * 128:(j + 1) * 128] = main.astype(BF16)
            out_tan[at, j * 128:(j + 1) * 128] = tan.astype(BF16)
        mean_square = jnp.sum(square, axis=1, keepdims=True) / width
        mean_cross = jnp.sum(cross, axis=1, keepdims=True) / width
        inv = lax.rsqrt(mean_square + 1e-05)
        inv_wide = jnp.broadcast_to(inv, (step_rows, 128))
        pull = jnp.broadcast_to(inv * inv * inv * mean_cross, (step_rows, 128))
        for j in range(pairs):
            lanes = slice(j * 128, (j + 1) * 128)
            by = gain[lanes].reshape(1, 128)
            main = out_main[at, lanes].astype(F32)
            tan = out_tan[at, lanes].astype(F32)
            out_main[at, lanes] = (by * main * inv_wide).astype(BF16)
            out_tan[at, lanes] = (by * (tan * inv_wide - main * pull)).astype(BF16)
        return carry

    for i in range(pieces):
        for h in range(heads):
            for o in order:
                g_copy(h, o, i).wait_recv()
        steps = span // step_rows
        lax.fori_loop(i * steps, (i + 1) * steps, norm, 0)

    for h in range(heads):
        for o in order:
            for i in range(pieces):
                g_copy(h, o, i).wait_send()
        for d in range(chain - 1, 0, -1):
            @pl.when(rank + d < chain)
            def _():
                s_copy(h, d, seq + d).wait_send()


def local(n_seq, n_head, xs, dxs, zgate, bmat, cmat, dt_raw, dt_bias, a_rate, d_skip, gain, traj_ids):
    tokens = xs.shape[0]
    heads = dt_raw.shape[0]
    blocks = tokens // Q
    rows = tokens // n_head
    width = xs.shape[1] * n_head
    chain = n_seq // 2
    vmem = pl.BlockSpec(memory_space=pltpu.VMEM)
    hbm = pl.BlockSpec(memory_space=pltpu.HBM)
    span = 128 if rows % 128 == 0 else rows
    return pl.pallas_call(
        functools.partial(kernel, n_seq, n_head, heads, blocks, rows),
        out_shape=[jax.ShapeDtypeStruct((rows, width), BF16)] * 2,
        in_specs=[hbm] * 11,
        out_specs=[vmem] * 2,
        scratch_shapes=[
            pltpu.VMEM((xs.shape[1], tokens), BF16),
            pltpu.VMEM((xs.shape[1], tokens), BF16),
            pltpu.VMEM((xs.shape[1], tokens), BF16),
            pltpu.VMEM(bmat.shape, BF16),
            pltpu.VMEM(cmat.shape, BF16),
            pltpu.VMEM(dt_raw.shape, F32),
            pltpu.SMEM(dt_bias.shape, F32),
            pltpu.SMEM(a_rate.shape, F32),
            pltpu.SMEM(d_skip.shape, F32),
            pltpu.VMEM(gain.shape, F32),
            pltpu.SMEM(traj_ids.shape, jnp.int32),
            pltpu.SemaphoreType.DMA((11,)),
            pltpu.VMEM((8, tokens), F32),
            pltpu.VMEM((heads, blocks, 128, 128), F32),
            pltpu.VMEM((blocks, 8, Q), F32),
            pltpu.VMEM((blocks, 8, Q), F32),
            pltpu.VMEM((blocks, 8, Q), F32),
            pltpu.VMEM((blocks, Q, 8), F32),
            pltpu.VMEM((blocks, 8, 128), F32),
            pltpu.VMEM((blocks, Q, Q), F32),
            pltpu.VMEM((blocks, 128, Q), F32),
            pltpu.VMEM((blocks, 64, Q), F32),
            pltpu.VMEM((heads, 128 + TAIL, 128), BF16),
            pltpu.VMEM((chain - 1, heads, 128 + TAIL, 128), BF16),
            pltpu.VMEM((128, 128), F32),
            pltpu.VMEM((heads, tokens, 128), BF16),
            pltpu.VMEM((n_head, heads, rows, 128), BF16),
            pltpu.SemaphoreType.DMA((chain - 1, heads)),
            pltpu.SemaphoreType.DMA((chain - 1, heads)),
            pltpu.SemaphoreType.DMA((n_head - 1, heads, rows // span)),
            pltpu.SemaphoreType.DMA((n_head - 1, heads, rows // span)),
            pltpu.SemaphoreType.DMA((heads,)),
        ],
        compiler_params=pltpu.CompilerParams(
            collective_id=0, has_side_effects=True, vmem_limit_bytes=56 * 2**20
        ),
        name="ssd_layer",
    )(xs.T, dxs.T, zgate.T, bmat, cmat, dt_raw, dt_bias, a_rate, d_skip, gain, traj_ids)


def solution(mesh):
    placed = (
        P("seq", "head"), P("seq", "head"), P("seq", "head"), P("seq", None), P("seq", None),
        P("head", "seq"), P("head"), P("head"), P("head"), P(), P("seq"),
    )
    return jax.shard_map(
        functools.partial(local, mesh.shape["seq"], mesh.shape["head"]),
        mesh=mesh,
        in_specs=placed,
        out_specs=(P(("seq", "head"), None), P(("seq", "head"), None)),
        check_vma=False,
    )
```

profile of v0, /device:TPU:0, one launch (start us, length us, event | category | flops | bytes accessed | tf_op | source)
XLA Modules:
  0.0 36.5 jit_solution(7711395299114620000)
XLA Ops:
  0.6 32.6 %ssd_layer.1 = (bf16[384,1280]{1,0:T(8,128)(2,1)}, bf16[384,1280]{1,0:T(8,128)(2,1)}) custom-call(bf16[320,1536]{1,0:T(8,128)(2,1)} %bitcast.3, bf16[320,1536]{1,0:T(8,128)(2,1)} %bitcast.4, bf16[320,1536]{1,0:T(8,128)(2,1)} %bitcast.5, bf16[1536,128]{1,0:T(8,128)(2,1)} %bm_hbm.1, bf16[1536,128]{1,0:T(8,128)(2,1)} %cm_hbm.1, f32[5,1536]{1,0:T(8,128)} %dt_hbm.1, ...), custom_call_target="tpu_custom_call" | custom-call | tf_op jit(solution)/shard_map/ssd_layer/pallas_call | solution.py:287
  33.3 0.0 copy-start
  33.3 2.3 %copy.15 = bf16[384,1280]{1,0:T(8,128)(2,1)} copy(bf16[384,1280]{1,0:T(8,128)(2,1)} %get-tuple-element.4) | data formatting | bytes 1966080
  35.6 0.0 copy-done
  35.6 0.9 %copy.16 = bf16[384,1280]{1,0:T(8,128)(2,1)} copy(bf16[384,1280]{1,0:T(8,128)(2,1)S(1)} %copy-done) | data formatting | bytes 1966080
Async XLA Ops:
  33.3 2.3 %copy-start = (bf16[384,1280]{1,0:T(8,128)(2,1)S(1)}, bf16[384,1280]{1,0:T(8,128)(2,1)}, u32[]{:S(2)}) copy-start(bf16[384,1280]{1,0:T(8,128)(2,1)} %get-tuple-element.5) | copy-start | bytes 2949124
where the time goes:
time: 36.7 us; the launch traced here: 36.5 us
  Pallas kernels  32.6 us (89%)
  local copies, waits for them, and re-layouts  3.24 us (9%)
  between operations  0.65 us (2%)
    pallas_call x1, Pallas kernels, local(): pl.pallas_call(functools.partial(kernel, n_seq, n_head, heads, blocks, ro...  32.6 us
    unnamed x4, local copies, waits for them, and re-layouts  3.24 us

commit v1 on v0

--- a/solution.py
+++ b/solution.py
@@ -32,7 +32,7 @@
     xs_hbm, dxs_hbm, zg_hbm, bm_hbm, cm_hbm, dt_hbm, bias_hbm, rate_hbm, skip_hbm, gain_hbm, traj_hbm,
     out_main, out_tan,
     xs, dxs, zg, bm, cm, dt, bias, rate, skip, gain, traj, in_sem,
-    dt8, bstate, lrow, wrow, erow, lcol, dec, table, part, scale, smsg, sgot, enter, gsend, got,
+    dt8, bstate, lrow, wrow, erow, lcol, dec, table, cmt, part, scale, smsg, sgot, enter, gsend, got,
     s_send, s_recv, g_send, g_recv, own_sem,
 ):
     chain = n_seq // 2
@@ -44,9 +44,11 @@
     fetches = [
         pltpu.make_async_copy(source, target, in_sem.at[i])
         for i, (source, target) in enumerate((
-            (dt_hbm, dt), (bias_hbm, bias), (rate_hbm, rate), (xs_hbm, xs), (dxs_hbm, dxs),
-            (bm_hbm, bm), (traj_hbm, traj), (cm_hbm, cm), (zg_hbm, zg), (skip_hbm, skip),
-            (gain_hbm, gain),
+            (dt_hbm, dt), (bias_hbm, bias), (rate_hbm, rate),
+            (xs_hbm.at[0:64], xs.at[0:64]), (dxs_hbm.at[0:64], dxs.at[0:64]),
+            (bm_hbm, bm), (traj_hbm, traj),
+            (xs_hbm.at[64:], xs.at[64:]), (dxs_hbm.at[64:], dxs.at[64:]),
+            (cm_hbm, cm), (zg_hbm, zg), (skip_hbm, skip), (gain_hbm, gain),
         ))
     ]
     for fetch in fetches:
@@ -113,6 +115,9 @@
     last_id = traj[blocks - 1].astype(F32)
     tail_row = lax.broadcasted_iota(jnp.int32, (TAIL, 128), 0)
     for h in range(heads):
+        if h == 1:
+            for fetch in fetches[7:9]:
+                fetch.wait()
         state = None
         for c in range(blocks):
             weighted = (values_of(h, c).astype(F32) * wrow[c, h:h + 1, :]).astype(BF16)
@@ -134,20 +139,21 @@
             def _():
                 s_copy(h, d, seq + d).start()
 
-    for fetch in fetches[7:]:
+    for fetch in fetches[9:]:
         fetch.wait()
     log_row = log_decay - jnp.log(step)
     decay = jnp.exp(log_decay)
-    turned = jnp.concatenate([log_decay, jnp.zeros((128 - blocks * 8, Q), F32)], axis=0).T
+    turned = jnp.concatenate([log_row, jnp.zeros((128 - blocks * 8, Q), F32)], axis=0).T
     row_at = lax.broadcasted_iota(jnp.int32, (Q, Q), 0)
     col_at = lax.broadcasted_iota(jnp.int32, (Q, Q), 1)
-    causal = row_at >= col_at
+    causal = row_at <= col_at
     for c in range(blocks):
-        lrow[c] = log_row[c * 8:(c + 1) * 8]
+        lrow[c] = log_decay[c * 8:(c + 1) * 8]
         erow[c] = decay[c * 8:(c + 1) * 8]
         lcol[c] = turned[:, c * 8:(c + 1) * 8]
         at = slice(c * Q, (c + 1) * Q)
-        table[c] = jnp.where(causal, by_rows(cm[at, :], bm[at, :]), 0.0)
+        table[c] = jnp.where(causal, by_rows(bm[at, :], cm[at, :]), 0.0)
+        cmt[c] = cm[at, :].astype(F32).T.astype(BF16)
 
     def g_copy(h, o, i):
         to = lax.rem(me + o, n_head)
@@ -178,16 +184,20 @@
             gate_in = zg[low:low + 64, at].astype(F32)
             gate = gate_in / (1.0 + jnp.exp(-gate_in))
             w_top = table[c, 0:HALF, 0:HALF] * jnp.exp(
-                jnp.minimum(wide[0:HALF] - row[:, 0:HALF], 4.0)
+                jnp.minimum(row[:, 0:HALF] - wide[0:HALF], 4.0)
             )
-            w_left = table[c, HALF:Q, 0:HALF] * jnp.exp(wide[HALF:Q] - row[:, 0:HALF])
+            w_right = table[c, 0:HALF, HALF:Q] * jnp.exp(row[:, HALF:Q] - wide[0:HALF])
             w_corner = table[c, HALF:Q, HALF:Q] * jnp.exp(
-                jnp.minimum(wide[HALF:Q] - row[:, HALF:Q], 4.0)
+                jnp.minimum(row[:, HALF:Q] - wide[HALF:Q], 4.0)
             )
-            w_low = jnp.concatenate([w_left.astype(BF16), w_corner.astype(BF16)], axis=1)
+            w_last = jnp.concatenate([w_right.astype(BF16), w_corner.astype(BF16)], axis=0)
             values = values_of(h, c)
             y = jnp.concatenate(
-                [by_rows(values[:, 0:HALF], w_top.astype(BF16)), by_rows(values, w_low)], axis=1
+                [
+                    jnp.dot(values[:, 0:HALF], w_top.astype(BF16), preferred_element_type=F32),
+                    jnp.dot(values, w_last, preferred_element_type=F32),
+                ],
+                axis=1,
             )
             y = y + skip[h] * values.astype(F32)
             part[c] = y * jnp.concatenate([gate, gate], axis=0)
@@ -205,10 +215,10 @@
         state = enter[...]
         for c in range(blocks):
             at = slice(c * Q, (c + 1) * Q)
-            carried = by_rows(state.astype(BF16), cm[at, :])
+            carried = jnp.dot(state.astype(BF16), cmt[c], preferred_element_type=F32)
             scaled = scale[c]
             gated = part[c] + carried * jnp.concatenate([scaled, scaled], axis=0)
-            gsend[h, at, :] = gated.T.astype(BF16)
+            gsend[h, at, :] = gated.astype(BF16).T
             if c < blocks - 1:
                 state = keep_after(c) * (dec[c, h:h + 1, :] * state + bstate[h, c])
         own_copy(h).start()
@@ -301,7 +311,7 @@
             pltpu.SMEM(d_skip.shape, F32),
             pltpu.VMEM(gain.shape, F32),
             pltpu.SMEM(traj_ids.shape, jnp.int32),
-            pltpu.SemaphoreType.DMA((11,)),
+            pltpu.SemaphoreType.DMA((13,)),
             pltpu.VMEM((8, tokens), F32),
             pltpu.VMEM((heads, blocks, 128, 128), F32),
             pltpu.VMEM((blocks, 8, Q), F32),
@@ -310,6 +320,7 @@
             pltpu.VMEM((blocks, Q, 8), F32),
             pltpu.VMEM((blocks, 8, 128), F32),
             pltpu.VMEM((blocks, Q, Q), F32),
+            pltpu.VMEM((blocks, 128, Q), BF16),
             pltpu.VMEM((blocks, 128, Q), F32),
             pltpu.VMEM((blocks, 64, Q), F32),
             pltpu.VMEM((heads, 128 + TAIL, 128), BF16),

time: 36.7 us -> 36.8 us (level)
  no operation moved by 1% of the time
where the time goes in v1:
time: 36.8 us; the launch traced here: 36.6 us
  Pallas kernels  32.7 us (89%)
  local copies, waits for them, and re-layouts  3.24 us (9%)
  between operations  0.65 us (2%)
    pallas_call x1, Pallas kernels, local(): pl.pallas_call(functools.partial(kernel, n_seq, n_head, heads, blocks, ro...  32.7 us
    unnamed x4, local copies, waits for them, and re-layouts  3.24 us

profile of v1, /device:TPU:0, one launch (start us, length us, event | category | flops | bytes accessed | tf_op | source)
XLA Modules:
  0.0 36.6 jit_solution(5516475277505219302)
XLA Ops:
  0.6 32.7 %ssd_layer.1 = (bf16[384,1280]{1,0:T(8,128)(2,1)}, bf16[384,1280]{1,0:T(8,128)(2,1)}) custom-call(bf16[320,1536]{1,0:T(8,128)(2,1)} %bitcast.3, bf16[320,1536]{1,0:T(8,128)(2,1)} %bitcast.4, bf16[320,1536]{1,0:T(8,128)(2,1)} %bitcast.5, bf16[1536,128]{1,0:T(8,128)(2,1)} %bm_hbm.1, bf16[1536,128]{1,0:T(8,128)(2,1)} %cm_hbm.1, f32[5,1536]{1,0:T(8,128)} %dt_hbm.1, ...), custom_call_target="tpu_custom_call" | custom-call | tf_op jit(solution)/shard_map/ssd_layer/pallas_call | solution.py:297
  33.4 0.0 copy-start
  33.4 2.3 %copy.15 = bf16[384,1280]{1,0:T(8,128)(2,1)} copy(bf16[384,1280]{1,0:T(8,128)(2,1)} %get-tuple-element.4) | data formatting | bytes 1966080
  35.7 0.0 copy-done
  35.7 0.9 %copy.16 = bf16[384,1280]{1,0:T(8,128)(2,1)} copy(bf16[384,1280]{1,0:T(8,128)(2,1)S(1)} %copy-done) | data formatting | bytes 1966080
Async XLA Ops:
  33.4 2.3 %copy-start = (bf16[384,1280]{1,0:T(8,128)(2,1)S(1)}, bf16[384,1280]{1,0:T(8,128)(2,1)}, u32[]{:S(2)}) copy-start(bf16[384,1280]{1,0:T(8,128)(2,1)} %get-tuple-element.5) | copy-start | bytes 2949124

commit v2 on v1

--- a/solution.py
+++ b/solution.py
@@ -29,10 +29,10 @@
 
 def kernel(
     n_seq, n_head, heads, blocks, rows,
-    xs_hbm, dxs_hbm, zg_hbm, bm_hbm, cm_hbm, dt_hbm, bias_hbm, rate_hbm, skip_hbm, gain_hbm, traj_hbm,
-    out_main, out_tan,
-    xs, dxs, zg, bm, cm, dt, bias, rate, skip, gain, traj, in_sem,
-    dt8, bstate, lrow, wrow, erow, lcol, dec, table, cmt, part, scale, smsg, sgot, enter, gsend, got,
+    xs_hbm, dxs_hbm, zg_hbm, bm_hbm, cm_hbm, dt_hbm, bias_hbm, rate_hbm, skip_hbm, traj_hbm,
+    got,
+    xs, dxs, zg, bm, cm, dt, bias, rate, skip, traj, in_sem,
+    dt8, bstate, lrow, wrow, erow, lcol, dec, table, cmt, part, scale, smsg, sgot, enter, gsend,
     s_send, s_recv, g_send, g_recv, own_sem,
 ):
     chain = n_seq // 2
@@ -48,7 +48,7 @@
             (xs_hbm.at[0:64], xs.at[0:64]), (dxs_hbm.at[0:64], dxs.at[0:64]),
             (bm_hbm, bm), (traj_hbm, traj),
             (xs_hbm.at[64:], xs.at[64:]), (dxs_hbm.at[64:], dxs.at[64:]),
-            (cm_hbm, cm), (zg_hbm, zg), (skip_hbm, skip), (gain_hbm, gain),
+            (cm_hbm, cm), (zg_hbm, zg), (skip_hbm, skip),
         ))
     ]
     for fetch in fetches:
@@ -155,13 +155,13 @@
         table[c] = jnp.where(causal, by_rows(bm[at, :], cm[at, :]), 0.0)
         cmt[c] = cm[at, :].astype(F32).T.astype(BF16)
 
-    def g_copy(h, o, i):
+    def g_copy(h, o):
         to = lax.rem(me + o, n_head)
         return pltpu.make_async_remote_copy(
-            src_ref=gsend.at[h, pl.ds(pl.multiple_of(to * rows + i * span, 16), span), :],
-            dst_ref=got.at[me, h, pl.ds(i * span, span), :],
-            send_sem=g_send.at[o - 1, h, i],
-            recv_sem=g_recv.at[o - 1, h, i],
+            src_ref=gsend.at[h, pl.ds(pl.multiple_of(to * rows, 16), rows), :],
+            dst_ref=got.at[me, h],
+            send_sem=g_send.at[o - 1, h],
+            recv_sem=g_recv.at[o - 1, h],
             device_id=(seq, to),
             device_id_type=MESH,
         )
@@ -171,8 +171,6 @@
             gsend.at[h, pl.ds(pl.multiple_of(me * rows, 16), rows), :], got.at[me, h], own_sem.at[h]
         )
 
-    span = 128 if rows % 128 == 0 else rows
-    pieces = rows // span
     order = sorted(range(1, n_head), key=lambda o: abs(o - n_head // 2))
     first_id = traj[0].astype(F32)
     for h in range(heads):
@@ -222,27 +220,29 @@
             if c < blocks - 1:
                 state = keep_after(c) * (dec[c, h:h + 1, :] * state + bstate[h, c])
         own_copy(h).start()
-        if h < heads - 2:
-            for o in order:
-                for i in range(pieces):
-                    g_copy(h, o, i).start()
-    for i in range(pieces):
-        for h in range(heads - 2, heads):
-            for o in order:
-                g_copy(h, o, i).start()
+        for o in order:
+            g_copy(h, o).start()
 
     for h in range(heads):
         own_copy(h).wait()
-
+        for o in order:
+            g_copy(h, o).wait()
+        for d in range(chain - 1, 0, -1):
+            @pl.when(rank + d < chain)
+            def _():
+                s_copy(h, d, seq + d).wait_send()
+
+
+def norm_kernel(heads, got, gain, out_main, out_tan):
+    n_head, _, rows, _ = got.shape
     pairs = n_head * heads // 2
     width = n_head * heads * 64
-    step_rows = 32
-    left_lanes = lax.broadcasted_iota(jnp.int32, (step_rows, 128), 1) < 64
-
-    def norm(i, carry):
-        at = pl.ds(pl.multiple_of(i * step_rows, step_rows), step_rows)
-        square = jnp.zeros((step_rows, 128), F32)
-        cross = jnp.zeros((step_rows, 128), F32)
+    span = 32
+    left_lanes = lax.broadcasted_iota(jnp.int32, (span, 128), 1) < 64
+    for i in range(rows // span):
+        at = slice(i * span, (i + 1) * span)
+        square = jnp.zeros((span, 128), F32)
+        cross = jnp.zeros((span, 128), F32)
         for j in range(pairs):
             k, m = 2 * j, 2 * j + 1
             one = got[k // heads, k % heads, at, :].astype(F32)
@@ -256,8 +256,8 @@
         mean_square = jnp.sum(square, axis=1, keepdims=True) / width
         mean_cross = jnp.sum(cross, axis=1, keepdims=True) / width
         inv = lax.rsqrt(mean_square + 1e-05)
-        inv_wide = jnp.broadcast_to(inv, (step_rows, 128))
-        pull = jnp.broadcast_to(inv * inv * inv * mean_cross, (step_rows, 128))
+        inv_wide = jnp.broadcast_to(inv, (span, 128))
+        pull = jnp.broadcast_to(inv * inv * inv * mean_cross, (span, 128))
         for j in range(pairs):
             lanes = slice(j * 128, (j + 1) * 128)
             by = gain[lanes].reshape(1, 128)
@@ -265,23 +265,6 @@
             tan = out_tan[at, lanes].astype(F32)
             out_main[at, lanes] = (by * main * inv_wide).astype(BF16)
             out_tan[at, lanes] = (by * (tan * inv_wide - main * pull)).astype(BF16)
-        return carry
-
-    for i in range(pieces):
-        for h in range(heads):
-            for o in order:
-                g_copy(h, o, i).wait_recv()
-        steps = span // step_rows
-        lax.fori_loop(i * steps, (i + 1) * steps, norm, 0)
-
-    for h in range(heads):
-        for o in order:
-            for i in range(pieces):
-                g_copy(h, o, i).wait_send()
-        for d in range(chain - 1, 0, -1):
-            @pl.when(rank + d < chain)
-            def _():
-                s_copy(h, d, seq + d).wait_send()
 
 
 def local(n_seq, n_head, xs, dxs, zgate, bmat, cmat, dt_raw, dt_bias, a_rate, d_skip, gain, traj_ids):
@@ -291,14 +274,12 @@
     rows = tokens // n_head
     width = xs.shape[1] * n_head
     chain = n_seq // 2
-    vmem = pl.BlockSpec(memory_space=pltpu.VMEM)
     hbm = pl.BlockSpec(memory_space=pltpu.HBM)
-    span = 128 if rows % 128 == 0 else rows
-    return pl.pallas_call(
+    got = pl.pallas_call(
         functools.partial(kernel, n_seq, n_head, heads, blocks, rows),
-        out_shape=[jax.ShapeDtypeStruct((rows, width), BF16)] * 2,
-        in_specs=[hbm] * 11,
-        out_specs=[vmem] * 2,
+        out_shape=jax.ShapeDtypeStruct((n_head, heads, rows, 128), BF16),
+        in_specs=[hbm] * 10,
+        out_specs=hbm,
         scratch_shapes=[
             pltpu.VMEM((xs.shape[1], tokens), BF16),
             pltpu.VMEM((xs.shape[1], tokens), BF16),
@@ -309,9 +290,8 @@
             pltpu.SMEM(dt_bias.shape, F32),
             pltpu.SMEM(a_rate.shape, F32),
             pltpu.SMEM(d_skip.shape, F32),
-            pltpu.VMEM(gain.shape, F32),
             pltpu.SMEM(traj_ids.shape, jnp.int32),
-            pltpu.SemaphoreType.DMA((13,)),
+            pltpu.SemaphoreType.DMA((12,)),
             pltpu.VMEM((8, tokens), F32),
             pltpu.VMEM((heads, blocks, 128, 128), F32),
             pltpu.VMEM((blocks, 8, Q), F32),
@@ -327,18 +307,30 @@
             pltpu.VMEM((chain - 1, heads, 128 + TAIL, 128), BF16),
             pltpu.VMEM((128, 128), F32),
             pltpu.VMEM((heads, tokens, 128), BF16),
-            pltpu.VMEM((n_head, heads, rows, 128), BF16),
             pltpu.SemaphoreType.DMA((chain - 1, heads)),
             pltpu.SemaphoreType.DMA((chain - 1, heads)),
-            pltpu.SemaphoreType.DMA((n_head - 1, heads, rows // span)),
-            pltpu.SemaphoreType.DMA((n_head - 1, heads, rows // span)),
+            pltpu.SemaphoreType.DMA((n_head - 1, heads)),
+            pltpu.SemaphoreType.DMA((n_head - 1, heads)),
             pltpu.SemaphoreType.DMA((heads,)),
         ],
         compiler_params=pltpu.CompilerParams(
             collective_id=0, has_side_effects=True, vmem_limit_bytes=56 * 2**20
         ),
         name="ssd_layer",
-    )(xs.T, dxs.T, zgate.T, bmat, cmat, dt_raw, dt_bias, a_rate, d_skip, gain, traj_ids)
+    )(xs.T, dxs.T, zgate.T, bmat, cmat, dt_raw, dt_bias, a_rate, d_skip, traj_ids)
+    part_rows = 96
+    return pl.pallas_call(
+        functools.partial(norm_kernel, heads),
+        grid=(rows // part_rows,),
+        out_shape=[jax.ShapeDtypeStruct((rows, width), BF16)] * 2,
+        in_specs=[
+            pl.BlockSpec((n_head, heads, part_rows, 128), lambda i: (0, 0, i, 0)),
+            pl.BlockSpec(gain.shape, lambda i: (0,)),
+        ],
+        out_specs=[pl.BlockSpec((part_rows, width), lambda i: (i, 0))] * 2,
+        compiler_params=pltpu.CompilerParams(vmem_limit_bytes=56 * 2**20),
+        name="norm",
+    )(got, gain)
 
 
 def solution(mesh):

time: 36.8 us -> 35.2 us (0.957); the launches traced: 36.6 us -> 34.6 us
  local copies, waits for them, and re-layouts: 3.24 us -> 0 us
  Pallas kernels: 32.7 us -> 34 us
    pallas_call x0 -> x1, Pallas kernels: none -> 4.85 us  [local(): pl.pallas_call(functools.partial(norm_kernel, heads), grid=(rows // part_...]
    pallas_call x1, Pallas kernels: 32.7 us -> 29.1 us  [local(): pl.pallas_call(functools.partial(kernel, n_seq, n_head, heads, blocks, ro...]
    unnamed x4 -> x0, local copies, waits for them, and re-layouts: 3.24 us -> none
where the time goes in v2:
time: 35.2 us; the launch traced here: 34.6 us
  Pallas kernels  34 us (97%)
  between operations  0.64 us (2%)
    pallas_call x1, Pallas kernels, local(): pl.pallas_call(functools.partial(kernel, n_seq, n_head, heads, blocks, ro...  29.1 us
    pallas_call x1, Pallas kernels, local(): pl.pallas_call(functools.partial(norm_kernel, heads), grid=(rows // part_...  4.85 us

profile of v2, /device:TPU:0, one launch (start us, length us, event | category | flops | bytes accessed | tf_op | source)
XLA Modules:
  0.0 34.6 jit_solution(13756329860383326657)
XLA Ops:
  0.6 29.1 %ssd_layer.1.got = bf16[4,5,384,128]{3,2,1,0:T(8,128)(2,1)} custom-call(bf16[320,1536]{1,0:T(8,128)(2,1)} %bitcast.3, bf16[320,1536]{1,0:T(8,128)(2,1)} %bitcast.4, bf16[320,1536]{1,0:T(8,128)(2,1)} %bitcast.5, bf16[1536,128]{1,0:T(8,128)(2,1)} %bm_hbm.1, bf16[1536,128]{1,0:T(8,128)(2,1)} %cm_hbm.1, f32[5,1536]{1,0:T(8,128)} %dt_hbm.1, f32[5]{0:T(128)} %bias_hbm.1, ...), custom_call_target="tpu_custom_call" | custom-call | tf_op jit(solution)/shard_map/ssd_layer/pallas_call | solution.py:278
  29.8 4.9 %norm.1 = (bf16[384,1280]{1,0:T(8,128)(2,1)}, bf16[384,1280]{1,0:T(8,128)(2,1)}) custom-call(bf16[4,5,384,128]{3,2,1,0:T(8,128)(2,1)} %ssd_layer.1.got, f32[1280]{0:T(1024)} %gain.1), custom_call_target="tpu_custom_call" | custom-call | tf_op jit(solution)/shard_map/norm/pallas_call | solution.py:322
